TPU v7x, 32 devices: a whole 2x2x4 slice. The times are simulated.
32 devices in a mesh: ctx: 8 (over z, y), head: 4 (over x, core).
Axes of the slice: x: 2, y: 2, z: 4, core: 2. Of those that a mesh axis runs over, the one named last changes fastest.
Arguments:
- queries: bfloat16 [2048, 2048], P('ctx', 'head'), may hold values from -34 to 34
- keys: bfloat16 [2048, 2048], P('ctx', 'head'), may hold values from -34 to 34
- values: bfloat16 [2048, 2048], P('ctx', 'head'), may hold values from -6 to 6
- output_grad: bfloat16 [2048, 4096], P('ctx', 'head'), may hold values from -6 to 6
- out_weight: bfloat16 [2048, 4096], P('head'), may hold values from -0.125 to 0.125
- random_blocks: int32 [16, 32, 3], replicated, may hold values from 0 to 31, as said below
- global_blocks: int32 [2], replicated, may hold values from 0 to 31, as said below
Outputs:
- output: bfloat16 [2048, 4096], P('ctx', 'head')
- query_grad: bfloat16 [2048, 2048], P('ctx', 'head')
- key_grad: bfloat16 [2048, 2048], P('ctx', 'head')
- value_grad: bfloat16 [2048, 2048], P('ctx', 'head')
Inputs may be any that keep to these rules, and one draw needn't show every extreme that they name: Every entry random_blocks[h, i, r] names a block j with j // 4 != i // 4. For each group of 4 heads (heads g * 4 to (g + 1) * 4 - 1) and each aligned run of 4 query blocks, the 48 entries name blocks of any one other run at most 7 times, and of some run exactly 7 times. `global_blocks`: the 2 entries are distinct, and one of them is the last block.
All inputs are finite; a program needn't handle non-finite values.
Results may differ from a plain program's by a relative error of at most 0.027.
Values may be sent and summed in bfloat16 or wider, within the bound.
A program may use at most 128 MiB of HBM per device.

v0:
```python
import jax
import jax.numpy as jnp
from jax import lax
from jax.sharding import PartitionSpec as P

HD = 128
BLK = 64
R = 3
G = 2


def with_halo(cells, sides, width):
    for axis, dim in sides:
        count = lax.axis_size(axis)
        ends = count - 1
        head = lax.slice_in_dim(cells, 0, width, axis=dim)
        tail = lax.slice_in_dim(cells, cells.shape[dim] - width, cells.shape[dim], axis=dim)
        cells = jnp.concatenate(
            [
                lax.ppermute(tail, axis, [(i, (i + 1) % count) for i in range(ends)]),
                cells,
                lax.ppermute(head, axis, [((i + 1) % count, i) for i in range(ends)]),
            ],
            axis=dim,
        )
    return cells


def send_plan(request_table, shards, blocks, my_shard):
    requests = request_table.shape[1]
    owners = request_table // blocks
    within = request_table % blocks
    request_ids = jnp.arange(requests, dtype=jnp.int32)
    earlier = (owners[:, :, None] == owners[:, None, :]) & (
        request_ids[None, None, :] < request_ids[None, :, None]
    )
    ranking = jnp.sum(earlier.astype(jnp.int32), axis=2)
    capacity = (requests + shards - 2) // (shards - 1)
    slot_ids = jnp.arange(capacity, dtype=jnp.int32)
    owned = (owners == my_shard)[:, None, :] & (ranking[:, None, :] == slot_ids[None, :, None])
    tile_ids = (request_ids // (blocks * R))[None, :] * blocks + within
    send_tiles = jnp.sum(jnp.where(owned, tile_ids[:, None, :], 0), axis=2).reshape(-1)
    send_alive = jnp.any(owned, axis=2).reshape(-1)
    my_owners = lax.dynamic_index_in_dim(owners, my_shard, 0, keepdims=False)
    my_ranks = lax.dynamic_index_in_dim(ranking, my_shard, 0, keepdims=False)
    return (send_tiles, send_alive, my_owners * capacity + my_ranks)


def pick_tiles(pair_tiles, send_tiles, blocks):
    return pair_tiles[send_tiles % blocks, :, send_tiles // blocks, :]


def pair_products(row_tiles, window, global_pairs, fetched, low_edge, high_edge):
    nearby = jnp.einsum(
        "nqhd,nwbhd->nhqwb",
        row_tiles,
        window[..., low_edge:high_edge],
        preferred_element_type=jnp.float32,
    )
    distant = jnp.einsum(
        "nqhd,gbhd->nhqgb",
        row_tiles,
        global_pairs[..., low_edge:high_edge],
        preferred_element_type=jnp.float32,
    )
    chance = jnp.einsum(
        "nqhd,hnrbd->nhqrb",
        row_tiles,
        fetched[..., low_edge:high_edge],
        preferred_element_type=jnp.float32,
    )
    return jnp.concatenate([nearby, distant, chance], axis=3)


def collect_rows(mixing, window, global_pairs, fetched, low_edge, high_edge):
    nearby = jnp.einsum(
        "nhqwb,nwbhd->nqhd",
        mixing[:, :, :, :3],
        window[..., low_edge:high_edge],
        preferred_element_type=jnp.float32,
    )
    distant = jnp.einsum(
        "nhqgb,gbhd->nqhd",
        mixing[:, :, :, 3 : 3 + G],
        global_pairs[..., low_edge:high_edge],
        preferred_element_type=jnp.float32,
    )
    chance = jnp.einsum(
        "nhqrb,hnrbd->nqhd",
        mixing[:, :, :, 3 + G :],
        fetched[..., low_edge:high_edge],
        preferred_element_type=jnp.float32,
    )
    return nearby + distant + chance


def tile_terms(mixing, row_tiles):
    nearby = jnp.einsum(
        "nhqwb,nqhd->nwbhd", mixing[:, :, :, :3], row_tiles, preferred_element_type=jnp.float32
    )
    distant = jnp.einsum(
        "nhqgb,nqhd->gbhd",
        mixing[:, :, :, 3 : 3 + G],
        row_tiles,
        preferred_element_type=jnp.float32,
    )
    chance = jnp.einsum(
        "nhqrb,nqhd->hnrbd", mixing[:, :, :, 3 + G :], row_tiles, preferred_element_type=jnp.float32
    )
    return (nearby, distant, chance)


def body(queries, keys, values, output_grad, out_weight, random_blocks, global_blocks):
    shards = lax.axis_size("ctx")
    my_shard = lax.axis_index("ctx")
    head_group = lax.axis_index("head")
    tok_local, width_local = queries.shape
    head_dim = HD
    heads_local = width_local // head_dim
    blocks = tok_local // BLK
    scaling = head_dim ** (-0.5)
    query_tiles = queries.reshape(blocks, BLK, heads_local, head_dim)
    pair_tiles = jnp.concatenate(
        [
            keys.reshape(blocks, BLK, heads_local, head_dim),
            values.reshape(blocks, BLK, heads_local, head_dim),
        ],
        axis=3,
    )
    head_table = lax.dynamic_slice_in_dim(random_blocks, head_group * heads_local, heads_local, 0)
    request_table = (
        head_table.reshape(heads_local, shards, blocks, R)
        .transpose(1, 0, 2, 3)
        .reshape(shards, heads_local * blocks * R)
    )
    send_tiles, send_alive, receive_rows = send_plan(request_table, shards, blocks, my_shard)
    received = lax.all_to_all(
        pick_tiles(pair_tiles, send_tiles, blocks), "ctx", split_axis=0, concat_axis=0, tiled=True
    )
    fetched = received[receive_rows].reshape(heads_local, blocks, R, BLK, 2 * head_dim)
    padded = with_halo(pair_tiles.reshape(tok_local, 2 * width_local), (("ctx", 0),), BLK)
    padded = padded.reshape(blocks + 2, BLK, heads_local, 2 * head_dim)
    window = jnp.stack([padded[offset : offset + blocks] for offset in range(3)], axis=1)
    global_owner = global_blocks // blocks
    global_local = global_blocks % blocks
    picked = pair_tiles[global_local]
    holding = jnp.where(
        (global_owner == my_shard)[:, None, None, None], picked.astype(jnp.float32), 0.0
    )
    global_pairs = lax.psum(holding, "ctx").astype(jnp.bfloat16)
    first_block = my_shard * blocks
    window_ids = first_block + jnp.arange(blocks)[:, None] + jnp.arange(3)[None, :] - 1
    inside = (window_ids >= 0) & (window_ids < blocks * shards)
    alive_mask = jnp.concatenate([inside, jnp.ones((blocks, G + R), dtype=bool)], axis=1)[
        :, None, None, :, None
    ]
    logits = jnp.where(
        alive_mask,
        pair_products(query_tiles, window, global_pairs, fetched, 0, head_dim) * scaling,
        -jnp.inf,
    )
    row_max = jnp.max(logits, axis=(3, 4))
    log_total = row_max + jnp.log(jnp.sum(jnp.exp(logits - row_max[..., None, None]), axis=(3, 4)))
    weights_full = jnp.exp(logits - log_total[..., None, None])
    weights_low = weights_full.astype(jnp.bfloat16)
    attended = collect_rows(
        weights_low, window, global_pairs, fetched, head_dim, 2 * head_dim
    ).astype(jnp.bfloat16)
    attended_flat = attended.reshape(tok_local, width_local)
    partial_value = jnp.dot(attended_flat, out_weight, preferred_element_type=jnp.float32)
    output = lax.psum_scatter(partial_value, "head", scatter_dimension=1, tiled=True).astype(
        jnp.bfloat16
    )
    grad_sum = lax.dot_general(
        lax.all_gather(output_grad, "head", axis=1, tiled=True),
        out_weight,
        (((1,), (1,)), ((), ())),
        preferred_element_type=jnp.float32,
    )
    grad_tiles = grad_sum.astype(jnp.bfloat16).reshape(blocks, BLK, heads_local, head_dim)
    delta_rows = jnp.sum(
        grad_tiles.astype(jnp.float32) * attended.astype(jnp.float32), axis=3
    ).transpose(0, 2, 1)
    products = pair_products(grad_tiles, window, global_pairs, fetched, head_dim, 2 * head_dim)
    logit_grad = (weights_full * (products - delta_rows[..., None, None])).astype(jnp.bfloat16)
    query_grad = (
        (collect_rows(logit_grad, window, global_pairs, fetched, 0, head_dim) * scaling)
        .astype(jnp.bfloat16)
        .reshape(tok_local, width_local)
    )
    key_nearby, key_distant, key_chance = tile_terms(logit_grad, query_tiles)
    value_nearby, value_distant, value_chance = tile_terms(weights_low, grad_tiles)
    nearby_terms = jnp.concatenate([key_nearby * scaling, value_nearby], axis=4)
    framed = sum(
        (
            jnp.pad(nearby_terms[:, offset], ((offset, 2 - offset), (0, 0), (0, 0), (0, 0)))
            for offset in range(3)
        )
    )
    edge_rows = jnp.concatenate([framed[0], framed[blocks + 1]], axis=0).reshape(
        2 * BLK, 2 * width_local
    )
    arrived = with_halo(edge_rows.astype(jnp.bfloat16), (("ctx", 0),), BLK).astype(edge_rows.dtype)
    local_grad = framed[1 : blocks + 1]
    local_grad = local_grad.at[0].add(arrived[:BLK].reshape(BLK, heads_local, 2 * head_dim))
    local_grad = local_grad.at[blocks - 1].add(
        arrived[3 * BLK :].reshape(BLK, heads_local, 2 * head_dim)
    )
    distant_terms = jnp.concatenate([key_distant * scaling, value_distant], axis=3)
    summed = lax.psum(distant_terms, "ctx")
    selector = (
        (global_owner == my_shard)[:, None] & (global_local[:, None] == jnp.arange(blocks)[None, :])
    ).astype(jnp.float32)
    local_grad = local_grad + jnp.einsum(
        "gn,gbhd->nbhd", selector, summed, precision=lax.Precision.HIGHEST
    )
    chance_terms = (
        jnp.concatenate([key_chance * scaling, value_chance], axis=4)
        .astype(jnp.bfloat16)
        .reshape(-1, BLK, 2 * head_dim)
    )
    outgoing_grads = (
        jnp.zeros((send_tiles.shape[0], BLK, 2 * head_dim), jnp.bfloat16)
        .at[receive_rows]
        .set(chance_terms)
    )
    returned = lax.all_to_all(outgoing_grads, "ctx", split_axis=0, concat_axis=0, tiled=True)
    segment_ids = jnp.where(send_alive, send_tiles, heads_local * blocks)
    gathered = jax.ops.segment_sum(
        returned.astype(jnp.float32), segment_ids, num_segments=heads_local * blocks + 1
    )[: heads_local * blocks]
    local_grad = local_grad + gathered.reshape(heads_local, blocks, BLK, 2 * head_dim).transpose(
        1, 2, 0, 3
    )
    key_grad = local_grad[..., :head_dim].astype(jnp.bfloat16).reshape(tok_local, width_local)
    value_grad = local_grad[..., head_dim:].astype(jnp.bfloat16).reshape(tok_local, width_local)
    return (output, query_grad, key_grad, value_grad)


def solution(mesh):
    placed = (
        P("ctx", "head"),
        P("ctx", "head"),
        P("ctx", "head"),
        P("ctx", "head"),
        P("head", None),
        P(),
        P(),
    )
    return jax.shard_map(
        body,
        mesh=mesh,
        in_specs=placed,
        out_specs=(P("ctx", "head"), P("ctx", "head"), P("ctx", "head"), P("ctx", "head")),
        check_vma=False,
    )
```

profile of v0, /device:TPU:0, one launch (start us, length us, event | category | flops | bytes accessed | tf_op | source)
XLA Modules:
  0.0 266.9 jit_solution(3460373470147299995)
XLA Ops:
  7.2 0.7 all-gather.2.cloned.1.call-update
  9.5 1.0 reshape.465
  10.6 1.0 reshape.466
  11.7 2.1 gather_fusion.1
  13.8 7.4 %all-to-all-start = ((bf16[56,64,256]{2,1,0:T(8,128)(2,1)}), bf16[56,64,256]{2,1,0:T(8,128)(2,1)}, u32[]{:S(2)}, u32[]{:S(2)}) async-start(bf16[56,64,256]{2,1,0:T(8,128)(2,1)} %gather_fusion.1), calls=%async_computation | async-start | bytes 3670016 | tf_op jit(solution)/shard_map/all_to_all | solution.py:137
  21.5 3.9 %collective-permute-start = (bf16[64,1024]{1,0:T(8,128)(2,1)S(1)}, bf16[64,1024]{1,0:T(8,128)(2,1)S(1)}, u32[]{:S(2)}, u32[]{:S(2)}) collective-permute-start(bf16[64,1024]{1,0:T(8,128)(2,1)S(1)} %bitcast.209), channel_id=1, source_target_pairs={{0,4},{4,8},{8,12},{12,16},{16,20},{20,24},{24,28},{1,5},{5,9},{9,... | collective-permute-start | bytes 393224 | tf_op jit(solution)/shard_map/ppermute | solution.py:20
  25.5 1.3 collective-permute-start.1
  26.9 0.6 gather_fusion
  27.7 69.8 %all-reduce.8 = bf16[2,64,4,256]{3,1,2,0:T(8,128)(2,1)S(1)} all-reduce(f32[2,64,4,256]{3,1,2,0:T(8,128)S(1)} %convert_select_fusion), channel_id=1, replica_groups=mesh['ctx'=8,'head'=4] {'ctx'}, use_global_device_ids=true, to_apply=%region_0.1 | all-reduce | flops 131072 | bytes 786432 | tf_op jit(solution)/shard_map/psum | solution.py:150
  97.5 0.7 fusion.100
  98.2 0.4 convolution_bitcast_fusion.3
  98.6 0.4 copy.156
  99.2 0.6 copy-done.22
  99.9 0.7 copy-done.23
  100.5 1.1 pad_maximum_fusion.4
  101.6 0.4 stack.12
  102.1 0.4 stack.14
  102.8 1.1 copy-done.6
  103.9 0.4 convolution_bitcast_fusion.1
  104.3 4.1 %convolution_convert_fusion.1 = bf16[256,512]{1,0:T(8,128)(2,1)S(1)} fusion(bf16[256,4096]{1,0:T(8,128)(2,1)} %all-gather.2.cloned.1.call-done, bf16[512,4096]{1,0:T(8,128)(2,1)} %param.15), kind=kOutput, calls=%fused_computation.40 | convolution fusion | flops 1073872896 | bytes 6553600 | tf_op jit(solution)/shard_map/dot_general | solution.py:174
  108.5 1.4 convolution_bitcast_fusion.2
  109.9 2.7 fusion.22
  112.5 3.4 %gather_fusion.2 = bf16[48,64,256]{2,1,0:T(8,128)(2,1)} fusion(bf16[56,64,256]{2,1,0:T(8,128)(2,1)} %all-to-all-done, s32[1024]{0:T(1024)S(1)} %pad_clamp_fusion), kind=kCustom, calls=%fused_computation.2 | custom fusion | bytes 3145920 | tf_op jit(solution)/shard_map/gather | solution.py:140
  115.9 1.6 fusion.96
  117.5 0.9 copy-done.12
  118.5 0.3 convolution_bitcast_fusion
  118.8 0.8 fusion.93
  119.6 1.3 exponential_reduce_fusion
  120.9 1.1 fusion.3
  122.3 0.4 convolution_bitcast_fusion.9
  122.7 0.4 convolution_bitcast_fusion.7
  123.2 0.4 fusion.25
  123.9 1.1 multiply_reduce_fusion
  125.0 0.4 copy-done.16
  125.3 1.5 fusion.2
  126.9 1.4 copy-done.2
  128.6 0.8 pad_maximum_fusion.5
  129.9 5.4 %fusion.34 = f32[256,4096]{1,0:T(8,128)} fusion(bf16[512,4096]{1,0:T(8,128)(2,1)} %param.15, bf16[32,8,4,128]{3,2,1,0:T(4,128)(2,1)S(1)} %bitcast.194), kind=kOutput, calls=%fused_computation.76 | convolution fusion | flops 1073741824 | bytes 8650752 | tf_op jit(solution)/shard_map/dot_general | solution.py:170
  135.4 1.6 copy-done.3
  136.9 0.3 multiply_convert_fusion
  137.3 1.2 copy-done.5
  138.7 0.3 convolution_convert_fusion
  139.0 1.4 pad_maximum_fusion.1
  140.4 1.5 broadcast_in_dim.82
  141.8 7.7 %scatter_fusion = bf16[56,64,256]{2,1,0:T(8,128)(2,1)} fusion(bf16[56,64,256]{2,1,0:T(8,128)(2,1)} %broadcast_in_dim.82, s32[48]{0:T(128)S(1)} %fusion.85, bf16[48,64,256]{2,1,0:T(8,128)(2,1)} %pad_maximum_fusion.1), kind=kCustom, calls=%fused_computation.3 | custom fusion | bytes 4718784 | tf_op jit(solution)/shard_map/scatter | solution.py:225
  149.5 4.5 %all-to-all-start.1 = ((bf16[56,64,256]{2,1,0:T(8,128)(2,1)}), bf16[56,64,256]{2,1,0:T(8,128)(2,1)}, u32[]{:S(2)}, u32[]{:S(2)}) async-start(bf16[56,64,256]{2,1,0:T(8,128)(2,1)} %scatter_fusion), calls=%async_computation.2 | async-start | bytes 3670016 | tf_op jit(solution)/shard_map/all_to_all | solution.py:227
  154.0 0.3 fusion.44
  154.4 0.3 multiply_bitcast_fusion
  155.5 4.1 %collective-permute-start.2 = (bf16[64,1024]{1,0:T(8,128)(2,1)S(1)}, bf16[64,1024]{1,0:T(8,128)(2,1)S(1)}, u32[]{:S(2)}, u32[]{:S(2)}) collective-permute-start(bf16[64,1024]{1,0:T(8,128)(2,1)S(1)} %bitcast.203), channel_id=1, source_target_pairs={{0,4},{4,8},{8,12},{12,16},{16,20},{20,24},{24,28},{1,5},{5,9},{9,... | collective-permute-start | bytes 393224 | tf_op jit(solution)/shard_map/ppermute | solution.py:20
  159.7 1.4 collective-permute-start.3
  161.2 0.4 convolution_bitcast_fusion.6
  161.6 0.4 convolution_bitcast_fusion.4
  162.7 0.7 copy.353
  163.5 6.2 %collective-permute-done.2 = bf16[64,1024]{1,0:T(8,128)(2,1)S(1)} collective-permute-done((bf16[64,1024]{1,0:T(8,128)(2,1)S(1)}, bf16[64,1024]{1,0:T(8,128)(2,1)S(1)}, u32[]{:S(2)}, u32[]{:S(2)}) %collective-permute-start.2) | collective-permute-done | bytes 131104 | tf_op jit(solution)/shard_map/ppermute | solution.py:20
  169.7 2.7 collective-permute-done.3
  172.7 1.0 fusion.38
  173.8 38.0 %all-reduce.7.cloned.1.call-done = f32[2,64,4,256]{3,1,2,0:T(8,128)} async-done(((f32[2,64,4,256]{3,1,2,0:T(8,128)}), f32[2,64,4,256]{3,1,2,0:T(8,128)}) %all-reduce.7.cloned.1.call-update) | async-done | bytes 524304 | tf_op jit(solution)/shard_map/psum | solution.py:210
  211.7 2.6 fusion.32
  214.3 3.8 %convert_element_type.63 = f32[56,64,256]{2,1,0:T(8,128)} convert(bf16[56,64,256]{2,1,0:T(8,128)(2,1)} %all-to-all-done.1) | non-fusion elementwise | flops 917504 | bytes 5505024 | tf_op jit(solution)/shard_map/convert_element_type | solution.py:230
  218.2 9.1 %scatter_fusion.1 = f32[17,64,256]{2,1,0:T(8,128)S(1)} fusion(f32[17,64,256]{2,1,0:T(8,128)S(1)} %broadcast_in_dim.80, s32[56]{0:T(128)S(1)} %get-tuple-element.53, f32[56,64,256]{2,1,0:T(8,128)} %convert_element_type.63), kind=kCustom, calls=%fused_computation.4 | custom fusion | flops 917504 | bytes 11010272 | tf_op jit(solution)/shard_map/scatter-add | solution.py:229
  227.4 0.8 fusion.16
  228.7 0.9 copy_bitcast_fusion
  229.6 28.7 %reduce-scatter.2.cloned.1.call-done = f32[256,1024]{1,0:T(8,128)} async-done(((f32[256,4096]{1,0:T(8,128)}), f32[256,1024]{1,0:T(8,128)}) %reduce-scatter.2.cloned.1.call-update) | async-done | bytes 1048592 | tf_op jit(solution)/shard_map/reduce_scatter | solution.py:171
  258.3 2.1 convert_element_type.56
  (116 shorter events, 7.0 us)
Async XLA Ops:
  7.2 0.8 copy-start
  7.2 97.1 %all-gather.2.cloned.1.call-start = ((), (), s32[]{:S(2)}) async-start(), calls=%async_computation.4 | async-start | bytes 2621440 | tf_op jit(solution)/shard_map/all_gather | solution.py:175
  13.8 13.0 %copy-start.24 = (s32[2]{0:T(128)S(1)}, s32[2]{0:T(128)}, u32[]{:S(2)}) copy-start(s32[2]{0:T(128)} %param.17) | copy-start | bytes 28
  13.8 13.0 %copy-start.21 = (bf16[256,512]{1,0:T(8,128)(2,1)S(1)}, bf16[256,512]{1,0:T(8,128)(2,1)}, u32[]{:S(2)}) copy-start(bf16[256,512]{1,0:T(8,128)(2,1)} %param.11) | copy-start | bytes 786436
  13.8 98.7 %all-to-all-start = ((bf16[56,64,256]{2,1,0:T(8,128)(2,1)}), bf16[56,64,256]{2,1,0:T(8,128)(2,1)}, u32[]{:S(2)}, u32[]{:S(2)}) async-start(bf16[56,64,256]{2,1,0:T(8,128)(2,1)} %gather_fusion.1), calls=%async_computation | async-start | bytes 3670016 | tf_op jit(solution)/shard_map/all_to_all | solution.py:137
  21.2 190.5 %all-reduce.7.cloned.1.call-start = ((), (), s32[]{:S(2)}) async-start(), calls=%async_computation.5 | async-start | bytes 1048576 | tf_op jit(solution)/shard_map/psum | solution.py:210
  21.5 77.7 %collective-permute-start = (bf16[64,1024]{1,0:T(8,128)(2,1)S(1)}, bf16[64,1024]{1,0:T(8,128)(2,1)S(1)}, u32[]{:S(2)}, u32[]{:S(2)}) collective-permute-start(bf16[64,1024]{1,0:T(8,128)(2,1)S(1)} %bitcast.209), channel_id=1, source_target_pairs={{0,4},{4,8},{8,12},{12,16},{16,20},{20,24},{24,28},{1,5},{5,9},{9,... | collective-permute-start | bytes 393224 | tf_op jit(solution)/shard_map/ppermute | solution.py:20
  25.5 73.7 %collective-permute-start.1 = (bf16[64,1024]{1,0:T(8,128)(2,1)S(1)}, bf16[64,1024]{1,0:T(8,128)(2,1)S(1)}, u32[]{:S(2)}, u32[]{:S(2)}) collective-permute-start(bf16[64,1024]{1,0:T(8,128)(2,1)S(1)} %bitcast.210), channel_id=1, source_target_pairs={{4,0},{8,4},{12,8},{16,12},{20,16},{24,20},{28,24},{5,1},{9,5},{13... | collective-permute-start | bytes 393224 | tf_op jit(solution)/shard_map/ppermute | solution.py:22
  26.9 75.8 %copy-start.9 = (bf16[4,64,4,128]{3,2,1,0:T(4,128)(2,1)}, bf16[4,64,4,128]{3,2,1,0:T(4,128)(2,1)S(1)}, u32[]{:S(2)}) copy-start(bf16[4,64,4,128]{3,2,1,0:T(4,128)(2,1)S(1)} %reshape.468) | copy-start | bytes 786436
  98.2 0.8 copy-start.18
  99.2 0.7 copy-start.22
  99.9 0.7 copy-start.23
  102.7 1.1 copy-start.6
  104.2 4.3 %copy-start.17 = (bf16[2,64,4,128]{3,1,2,0:T(8,128)(2,1)S(1)}, bf16[2,64,4,128]{3,1,2,0:T(8,128)(2,1)}, u32[]{:S(2)}) copy-start(bf16[2,64,4,128]{3,1,2,0:T(8,128)(2,1)} %get-tuple-element.51) | copy-start | bytes 393220
  115.9 2.5 copy-start.10
  117.5 0.9 copy-start.12
  120.9 1.4 copy-start.7
  122.3 1.5 copy-start.4
  123.5 1.4 copy-start.14
  123.5 1.8 copy-start.16
  126.9 1.4 copy-start.2
  128.3 1.4 copy-start.20
  129.4 128.8 %reduce-scatter.2.cloned.1.call-start = ((), (), s32[]{:S(2)}) async-start(), calls=%async_computation.3 | async-start | bytes 5242880 | tf_op jit(solution)/shard_map/reduce_scatter | solution.py:171
  135.3 1.6 copy-start.3
  135.3 1.6 copy-start.11
  136.9 1.6 copy-start.5
  149.5 64.8 %all-to-all-start.1 = ((bf16[56,64,256]{2,1,0:T(8,128)(2,1)}), bf16[56,64,256]{2,1,0:T(8,128)(2,1)}, u32[]{:S(2)}, u32[]{:S(2)}) async-start(bf16[56,64,256]{2,1,0:T(8,128)(2,1)} %scatter_fusion), calls=%async_computation.2 | async-start | bytes 3670016 | tf_op jit(solution)/shard_map/all_to_all | solution.py:227
  155.0 6.2 %copy-start.8 = (bf16[4,3,64,4,256]{4,2,1,3,0:T(8,128)(2,1)S(1)}, bf16[4,3,64,4,256]{4,2,1,3,0:T(8,128)(2,1)}, u32[]{:S(2)}) copy-start(bf16[4,3,64,4,256]{4,2,1,3,0:T(8,128)(2,1)} %copy-done.6) | copy-start | bytes 4718596
  155.3 7.1 %copy-start.15 = (f32[6,64,4,256]{3,1,2,0:T(8,128)}, f32[6,64,4,256]{3,1,2,0:T(8,128)S(1)}, u32[]{:S(2)}) copy-start(f32[6,64,4,256]{3,1,2,0:T(8,128)S(1)} %get-tuple-element.29) | copy-start | bytes 4718596
  155.3 6.3 %copy-start.13 = (bf16[4,4,3,64,128]{4,3,2,1,0:T(8,128)(2,1)S(1)}, bf16[4,4,3,64,128]{4,3,2,1,0:T(8,128)(2,1)}, u32[]{:S(2)}) copy-start(bf16[4,4,3,64,128]{4,3,2,1,0:T(8,128)(2,1)} %copy-done.12) | copy-start | bytes 2359300
  155.5 14.2 %collective-permute-start.2 = (bf16[64,1024]{1,0:T(8,128)(2,1)S(1)}, bf16[64,1024]{1,0:T(8,128)(2,1)S(1)}, u32[]{:S(2)}, u32[]{:S(2)}) collective-permute-start(bf16[64,1024]{1,0:T(8,128)(2,1)S(1)} %bitcast.203), channel_id=1, source_target_pairs={{0,4},{4,8},{8,12},{12,16},{16,20},{20,24},{24,28},{1,5},{5,9},{9,... | collective-permute-start | bytes 393224 | tf_op jit(solution)/shard_map/ppermute | solution.py:20
  159.7 2.3 copy-start.19
  159.7 12.6 %collective-permute-start.3 = (bf16[64,1024]{1,0:T(8,128)(2,1)S(1)}, bf16[64,1024]{1,0:T(8,128)(2,1)S(1)}, u32[]{:S(2)}, u32[]{:S(2)}) collective-permute-start(bf16[64,1024]{1,0:T(8,128)(2,1)S(1)} %bitcast.205), channel_id=1, source_target_pairs={{4,0},{8,4},{12,8},{16,12},{20,16},{24,20},{28,24},{5,1},{9,5},{13... | collective-permute-start | bytes 393224 | tf_op jit(solution)/shard_map/ppermute | solution.py:22
  228.1 32.2 %copy-start.1 = (s32[16,32,3]{1,0,2:T(8,128)S(1)}, s32[16,32,3]{1,0,2:T(8,128)}, u32[]{:S(2)}) copy-start(s32[16,32,3]{1,0,2:T(8,128)} %param.16) | copy-start | bytes 18436
Sparse Core Ops, SparseCore 0:
  9.6 25.2 all-gather.1
  129.6 82.1 all-reduce.6
  214.4 43.7 reduce-scatter.1
where the time goes:
time: 268 us; the launch traced here: 267 us
  waiting for transfers between devices  76.3 us (28%)
  blocking collectives  69.8 us (26%)
  local copies, waits for them, and re-layouts  34 us (13%)
  other arithmetic  26.7 us (10%)
  starting transfers between devices  22.9 us (9%)
  matrix products  22.6 us (8%)
  between operations  14.6 us (5%)
    psum x1, blocking collectives, body(): global_pairs = lax.psum(holding, 'ctx').astype(jnp.bfloat16)  69.8 us
    psum x1, waiting for transfers between devices, body(): summed = lax.psum(distant_terms, 'ctx')  38 us
    reduce_scatter x1, waiting for transfers between devices, body(): lax.psum_scatter(partial_value, 'head', scatter_dimension=1, tiled=True)  28.7 us
    unnamed x57, local copies, waits for them, and re-layouts  9.25 us
    scatter-add x1, other arithmetic, body(): jax.ops.segment_sum(returned.astype(jnp.float32), segment_ids, num_segmen...  9.06 us
    ppermute x2, starting transfers between devices, with_halo(): lax.ppermute(tail, axis, [(i, (i + 1) % count) for i in range(ends)])  7.94 us
    scatter x1, local copies, waits for them, and re-layouts, body(): outgoing_grads = jnp.zeros((send_tiles.shape[0], BLK, 2 * head_dim), jnp....  7.68 us
    all_to_all x1, starting transfers between devices, body(): lax.all_to_all(pick_tiles(pair_tiles, send_tiles, blocks), 'ctx', split_a...  7.41 us
  transfers between devices with their start and end apart: 9, of which 4 were waited for; matrix products, arithmetic and copies ran while one was open for 22% of the time, Pallas kernels for 0%

commit v1 on v0

--- a/solution.py
+++ b/solution.py
@@ -147,7 +147,7 @@
     holding = jnp.where(
         (global_owner == my_shard)[:, None, None, None], picked.astype(jnp.float32), 0.0
     )
-    global_pairs = lax.psum(holding, "ctx").astype(jnp.bfloat16)
+    global_pairs = jnp.sum(lax.all_gather(holding, "ctx"), axis=0).astype(jnp.bfloat16)
     first_block = my_shard * blocks
     window_ids = first_block + jnp.arange(blocks)[:, None] + jnp.arange(3)[None, :] - 1
     inside = (window_ids >= 0) & (window_ids < blocks * shards)

time: 268 us -> 282 us (1.052)
  waiting for transfers between devices: 76.3 us -> 157 us
  blocking collectives: 69.8 us -> 0 us
  other arithmetic: 26.7 us -> 31.4 us
    psum x1 -> x0, blocking collectives: 69.8 us -> none  [body(): global_pairs = lax.psum(holding, 'ctx').astype(jnp.bfloat16)]
    all_gather x0 -> x1, waiting for transfers between devices: none -> 36.3 us  [body(): lax.all_gather(holding, 'ctx')]
    all_to_all x1, waiting for transfers between devices: 0.01 us -> 29.8 us  [body(): lax.all_to_all(pick_tiles(pair_tiles, send_tiles, blocks), 'ctx', split_a...]
    ppermute x2, waiting for transfers between devices: 6.24 us -> 22.9 us  [with_halo(): lax.ppermute(tail, axis, [(i, (i + 1) % count) for i in range(ends)])]
    reduce_sum x0 -> x1, other arithmetic: none -> 3.26 us  [body(): jnp.sum(lax.all_gather(holding, 'ctx'), axis=0).astype(jnp.bfloat16)]
  transfers between devices with their start and end apart: 9 -> 10, of which waited for: 4 -> 6; matrix products, arithmetic and copies ran while one was open for 22% -> 23% of each run, Pallas kernels for 0% -> 0%
where the time goes in v1:
time: 282 us; the launch traced here: 281 us
  waiting for transfers between devices  157 us (56%)
  local copies, waits for them, and re-layouts  32.3 us (11%)
  other arithmetic  31.4 us (11%)
  matrix products  23.5 us (8%)
  starting transfers between devices  22.5 us (8%)
  between operations  14.6 us (5%)
    psum x1, waiting for transfers between devices, body(): summed = lax.psum(distant_terms, 'ctx')  38.4 us
    all_gather x1, waiting for transfers between devices, body(): lax.all_gather(holding, 'ctx')  36.3 us
    all_to_all x1, waiting for transfers between devices, body(): lax.all_to_all(pick_tiles(pair_tiles, send_tiles, blocks), 'ctx', split_a...  29.8 us
    reduce_scatter x1, waiting for transfers between devices, body(): lax.psum_scatter(partial_value, 'head', scatter_dimension=1, tiled=True)  28.6 us
    ppermute x2, waiting for transfers between devices, with_halo(): lax.ppermute(tail, axis, [(i, (i + 1) % count) for i in range(ends)])  22.9 us
    scatter-add x1, other arithmetic, body(): jax.ops.segment_sum(returned.astype(jnp.float32), segment_ids, num_segmen...  8.97 us
    unnamed x57, local copies, waits for them, and re-layouts  8.2 us
    ppermute x2, starting transfers between devices, with_halo(): lax.ppermute(tail, axis, [(i, (i + 1) % count) for i in range(ends)])  7.81 us
  transfers between devices with their start and end apart: 10, of which 6 were waited for; matrix products, arithmetic and copies ran while one was open for 23% of the time, Pallas kernels for 0%

profile of v1, /device:TPU:0, one launch (start us, length us, event | category | flops | bytes accessed | tf_op | source)
XLA Modules:
  0.0 281.1 jit_solution(13441807569586002317)
XLA Ops:
  7.2 0.7 all-gather.5.cloned.1.call-update
  8.0 1.0 reshape.477
  9.0 1.0 reshape.478
  10.0 0.7 compare_select_fusion.3
  10.9 0.6 gather_fusion
  11.5 0.9 convert_select_fusion
  14.0 2.1 gather_fusion.1
  16.1 7.3 %all-to-all-start = ((bf16[56,64,256]{2,1,0:T(8,128)(2,1)}), bf16[56,64,256]{2,1,0:T(8,128)(2,1)}, u32[]{:S(2)}, u32[]{:S(2)}) async-start(bf16[56,64,256]{2,1,0:T(8,128)(2,1)} %gather_fusion.1), calls=%async_computation | async-start | bytes 3670016 | tf_op jit(solution)/shard_map/all_to_all | solution.py:137
  23.6 3.9 %collective-permute-start = (bf16[64,1024]{1,0:T(8,128)(2,1)S(1)}, bf16[64,1024]{1,0:T(8,128)(2,1)S(1)}, u32[]{:S(2)}, u32[]{:S(2)}) collective-permute-start(bf16[64,1024]{1,0:T(8,128)(2,1)S(1)} %bitcast.205), channel_id=1, source_target_pairs={{0,4},{4,8},{8,12},{12,16},{16,20},{20,24},{24,28},{1,5},{5,9},{9,... | collective-permute-start | bytes 393224 | tf_op jit(solution)/shard_map/ppermute | solution.py:20
  27.6 1.3 collective-permute-start.1
  29.0 0.4 copy.199
  29.5 0.8 reshape.480
  30.4 13.1 %collective-permute-done = bf16[64,1024]{1,0:T(8,128)(2,1)S(1)} collective-permute-done((bf16[64,1024]{1,0:T(8,128)(2,1)S(1)}, bf16[64,1024]{1,0:T(8,128)(2,1)S(1)}, u32[]{:S(2)}, u32[]{:S(2)}) %collective-permute-start) | collective-permute-done | bytes 131104 | tf_op jit(solution)/shard_map/ppermute | solution.py:20
  43.6 0.4 stack.12
  44.0 0.9 copy.201
  44.9 0.4 stack.14
  45.3 1.2 pad_maximum_fusion
  46.6 0.4 convolution_bitcast_fusion.1
  47.0 5.0 %convolution_convert_fusion.1 = bf16[256,512]{1,0:T(8,128)(2,1)} fusion(bf16[256,4096]{1,0:T(8,128)(2,1)} %all-gather.5.cloned.1.call-done, bf16[512,4096]{1,0:T(8,128)(2,1)} %param.15), kind=kOutput, calls=%fused_computation.40 | convolution fusion | flops 1073872896 | bytes 6553600 | tf_op jit(solution)/shard_map/dot_general | solution.py:174
  51.9 1.0 reshape.486
  53.0 1.6 fusion.22
  54.6 29.8 %all-to-all-done = bf16[56,64,256]{2,1,0:T(8,128)(2,1)} async-done(((bf16[56,64,256]{2,1,0:T(8,128)(2,1)}), bf16[56,64,256]{2,1,0:T(8,128)(2,1)}, u32[]{:S(2)}, u32[]{:S(2)}) %all-to-all-start) | async-done | bytes 1835040 | tf_op jit(solution)/shard_map/all_to_all | solution.py:137
  84.4 2.2 gather_fusion.2
  86.6 0.5 fusion.88
  87.0 0.9 copy-done.9
  87.9 0.3 convolution_bitcast_fusion
  88.3 1.5 fusion.25
  89.8 36.3 %all-gather.3.cloned.1.call-done = f32[8,2,64,4,256]{4,2,3,1,0:T(8,128)} async-done(((f32[1,2,64,4,256]{4,2,3,1,0:T(8,128)}), f32[8,2,64,4,256]{4,2,3,1,0:T(8,128)}) %all-gather.3.cloned.1.call-update) | async-done | bytes 4194320 | tf_op jit(solution)/shard_map/all_gather | solution.py:150
  126.0 3.3 %reduce_sum.45 = bf16[2,64,4,256]{3,1,2,0:T(8,128)(2,1)} reduce(f32[8,2,64,4,256]{4,2,3,1,0:T(8,128)} %all-gather.3.cloned.1.call-done, f32[]{:T(128)} %constant.164.clone.1), dimensions={0}, to_apply=%region_0.1 | reduce | flops 917504 | bytes 4456452 | tf_op jit(solution)/shard_map/reduce_sum | solution.py:150
  129.3 1.4 convolution_bitcast_fusion.3
  130.7 0.8 fusion.85
  131.5 1.2 exponential_reduce_fusion
  132.8 1.1 fusion.3
  134.2 0.4 convolution_bitcast_fusion.9
  134.6 1.2 copy-done.12
  135.9 0.4 convolution_bitcast_fusion.7
  136.3 0.4 convolution_bitcast_fusion.2
  137.0 1.1 multiply_reduce_fusion
  138.1 0.6 copy-done.18
  138.7 1.5 fusion.2
  140.3 1.4 copy-done.7
  142.0 0.8 pad_maximum_fusion.5
  143.3 5.4 %fusion.35 = f32[256,4096]{1,0:T(8,128)} fusion(bf16[512,4096]{1,0:T(8,128)(2,1)} %param.15, bf16[32,8,4,128]{3,2,1,0:T(4,128)(2,1)S(1)} %bitcast.190), kind=kOutput, calls=%fused_computation.78 | convolution fusion | flops 1073741824 | bytes 8650752 | tf_op jit(solution)/shard_map/dot_general | solution.py:170
  148.7 1.6 copy-done.8
  150.6 1.2 copy-done.3
  152.4 1.4 pad_maximum_fusion.1
  153.7 1.5 broadcast_in_dim.82
  155.2 7.6 %scatter_fusion = bf16[56,64,256]{2,1,0:T(8,128)(2,1)} fusion(bf16[56,64,256]{2,1,0:T(8,128)(2,1)} %broadcast_in_dim.82, s32[48]{0:T(128)S(1)} %fusion.76, bf16[48,64,256]{2,1,0:T(8,128)(2,1)} %pad_maximum_fusion.1), kind=kCustom, calls=%fused_computation.3 | custom fusion | bytes 4718784 | tf_op jit(solution)/shard_map/scatter | solution.py:225
  162.8 4.4 %all-to-all-start.1 = ((bf16[56,64,256]{2,1,0:T(8,128)(2,1)}), bf16[56,64,256]{2,1,0:T(8,128)(2,1)}, u32[]{:S(2)}, u32[]{:S(2)}) async-start(bf16[56,64,256]{2,1,0:T(8,128)(2,1)} %scatter_fusion), calls=%async_computation.2 | async-start | bytes 3670016 | tf_op jit(solution)/shard_map/all_to_all | solution.py:227
  168.7 3.9 %collective-permute-start.2 = (bf16[64,1024]{1,0:T(8,128)(2,1)S(1)}, bf16[64,1024]{1,0:T(8,128)(2,1)S(1)}, u32[]{:S(2)}, u32[]{:S(2)}) collective-permute-start(bf16[64,1024]{1,0:T(8,128)(2,1)S(1)} %bitcast.199), channel_id=1, source_target_pairs={{0,4},{4,8},{8,12},{12,16},{16,20},{20,24},{24,28},{1,5},{5,9},{9,... | collective-permute-start | bytes 393224 | tf_op jit(solution)/shard_map/ppermute | solution.py:20
  172.8 1.4 collective-permute-start.3
  174.2 0.4 convolution_bitcast_fusion.6
  174.7 0.4 convolution_bitcast_fusion.4
  175.8 0.7 copy.391
  176.5 9.8 %collective-permute-done.2 = bf16[64,1024]{1,0:T(8,128)(2,1)S(1)} collective-permute-done((bf16[64,1024]{1,0:T(8,128)(2,1)S(1)}, bf16[64,1024]{1,0:T(8,128)(2,1)S(1)}, u32[]{:S(2)}, u32[]{:S(2)}) %collective-permute-start.2) | collective-permute-done | bytes 131104 | tf_op jit(solution)/shard_map/ppermute | solution.py:20
  186.6 1.0 fusion.39
  187.7 38.4 %all-reduce.6.cloned.1.call-done = f32[2,64,4,256]{3,1,0,2:T(8,128)} async-done(((f32[2,64,4,256]{3,1,0,2:T(8,128)}), f32[2,64,4,256]{3,1,0,2:T(8,128)}) %all-reduce.6.cloned.1.call-update) | async-done | bytes 524304 | tf_op jit(solution)/shard_map/psum | solution.py:210
  226.1 2.6 fusion.33
  228.7 3.8 %convert_element_type.74 = f32[56,64,256]{2,1,0:T(8,128)} convert(bf16[56,64,256]{2,1,0:T(8,128)(2,1)} %all-to-all-done.1) | non-fusion elementwise | flops 917504 | bytes 5505024 | tf_op jit(solution)/shard_map/convert_element_type | solution.py:230
  232.6 9.0 %scatter_fusion.1 = f32[17,64,256]{2,1,0:T(8,128)S(1)} fusion(f32[17,64,256]{2,1,0:T(8,128)S(1)} %broadcast_in_dim.80, s32[56]{0:T(128)S(1)} %get-tuple-element.51, f32[56,64,256]{2,1,0:T(8,128)} %convert_element_type.74), kind=kCustom, calls=%fused_computation.4 | custom fusion | flops 917504 | bytes 11010272 | tf_op jit(solution)/shard_map/scatter-add | solution.py:229
  241.6 0.8 fusion.16
  243.0 0.9 copy_bitcast_fusion
  243.8 28.6 %reduce-scatter.2.cloned.1.call-done = f32[256,1024]{1,0:T(8,128)} async-done(((f32[256,4096]{1,0:T(8,128)}), f32[256,1024]{1,0:T(8,128)}) %reduce-scatter.2.cloned.1.call-update) | async-done | bytes 1048592 | tf_op jit(solution)/shard_map/reduce_scatter | solution.py:171
  272.5 2.1 convert_element_type.67
  (118 shorter events, 8.0 us)
Async XLA Ops:
  7.2 5.2 %copy-start = (s32[16,32,3]{1,0,2:T(8,128)S(1)}, s32[16,32,3]{1,0,2:T(8,128)}, u32[]{:S(2)}) copy-start(s32[16,32,3]{1,0,2:T(8,128)} %param.16) | copy-start | bytes 18436
  7.2 4.2 %copy-start.24 = (s32[2]{0:T(128)S(1)}, s32[2]{0:T(128)}, u32[]{:S(2)}) copy-start(s32[2]{0:T(128)} %param.17) | copy-start | bytes 28
  7.2 39.8 %all-gather.5.cloned.1.call-start = ((), (), s32[]{:S(2)}) async-start(), calls=%async_computation.5 | async-start | bytes 2621440 | tf_op jit(solution)/shard_map/all_gather | solution.py:175
  7.9 118.1 %all-gather.3.cloned.1.call-start = ((), (), s32[]{:S(2)}) async-start(), calls=%async_computation.3 | async-start | bytes 4718592 | tf_op jit(solution)/shard_map/all_gather | solution.py:150
  16.1 68.3 %all-to-all-start = ((bf16[56,64,256]{2,1,0:T(8,128)(2,1)}), bf16[56,64,256]{2,1,0:T(8,128)(2,1)}, u32[]{:S(2)}, u32[]{:S(2)}) async-start(bf16[56,64,256]{2,1,0:T(8,128)(2,1)} %gather_fusion.1), calls=%async_computation | async-start | bytes 3670016 | tf_op jit(solution)/shard_map/all_to_all | solution.py:137
  23.4 6.1 %copy-start.23 = (bf16[256,512]{1,0:T(8,128)(2,1)S(1)}, bf16[256,512]{1,0:T(8,128)(2,1)}, u32[]{:S(2)}) copy-start(bf16[256,512]{1,0:T(8,128)(2,1)} %param.11) | copy-start | bytes 786436
  23.4 202.7 %all-reduce.6.cloned.1.call-start = ((), (), s32[]{:S(2)}) async-start(), calls=%async_computation.6 | async-start | bytes 1048576 | tf_op jit(solution)/shard_map/psum | solution.py:210
  23.6 19.8 %collective-permute-start = (bf16[64,1024]{1,0:T(8,128)(2,1)S(1)}, bf16[64,1024]{1,0:T(8,128)(2,1)S(1)}, u32[]{:S(2)}, u32[]{:S(2)}) collective-permute-start(bf16[64,1024]{1,0:T(8,128)(2,1)S(1)} %bitcast.205), channel_id=1, source_target_pairs={{0,4},{4,8},{8,12},{12,16},{16,20},{20,24},{24,28},{1,5},{5,9},{9,... | collective-permute-start | bytes 393224 | tf_op jit(solution)/shard_map/ppermute | solution.py:20
  27.6 15.8 %collective-permute-start.1 = (bf16[64,1024]{1,0:T(8,128)(2,1)S(1)}, bf16[64,1024]{1,0:T(8,128)(2,1)S(1)}, u32[]{:S(2)}, u32[]{:S(2)}) collective-permute-start(bf16[64,1024]{1,0:T(8,128)(2,1)S(1)} %bitcast.206), channel_id=1, source_target_pairs={{4,0},{8,4},{12,8},{16,12},{20,16},{24,20},{28,24},{5,1},{9,5},{13... | collective-permute-start | bytes 393224 | tf_op jit(solution)/shard_map/ppermute | solution.py:22
  45.2 1.3 copy-start.13
  46.6 6.4 %copy-start.4 = (bf16[4,3,64,4,256]{4,2,1,3,0:T(8,128)(2,1)}, bf16[4,3,64,4,256]{4,2,1,3,0:T(8,128)(2,1)S(1)}, u32[]{:S(2)}) copy-start(bf16[4,3,64,4,256]{4,2,1,3,0:T(8,128)(2,1)S(1)} %pad_maximum_fusion) | copy-start | bytes 4718596
  86.5 1.4 copy-start.14
  87.0 0.9 copy-start.9
  87.0 1.2 copy-start.11
  132.8 1.4 copy-start.5
  134.2 2.8 %copy-start.2 = (bf16[4,4,64,8,64]{2,4,3,1,0:T(8,128)(2,1)}, bf16[4,4,64,8,64]{2,4,3,1,0:T(8,128)(2,1)S(1)}, u32[]{:S(2)}) copy-start(bf16[4,4,64,8,64]{2,4,3,1,0:T(8,128)(2,1)S(1)} %fusion.3) | copy-start | bytes 3145732
  134.2 1.7 copy-start.12
  134.2 2.1 copy-start.20
  136.7 1.4 copy-start.17
  136.7 2.0 copy-start.18
  138.7 2.9 %copy-start.15 = (bf16[4,64,4,128]{3,2,1,0:T(4,128)(2,1)S(1)}, bf16[4,64,4,128]{3,2,1,0:T(4,128)(2,1)}, u32[]{:S(2)}) copy-start(bf16[4,64,4,128]{3,2,1,0:T(4,128)(2,1)} %reshape.480) | copy-start | bytes 786436
  140.2 1.4 copy-start.7
  141.6 1.4 copy-start.22
  142.8 129.7 %reduce-scatter.2.cloned.1.call-start = ((), (), s32[]{:S(2)}) async-start(), calls=%async_computation.4 | async-start | bytes 5242880 | tf_op jit(solution)/shard_map/reduce_scatter | solution.py:171
  148.7 1.6 copy-start.8
  148.7 1.6 copy-start.16
  150.3 1.6 copy-start.3
  162.8 65.9 %all-to-all-start.1 = ((bf16[56,64,256]{2,1,0:T(8,128)(2,1)}), bf16[56,64,256]{2,1,0:T(8,128)(2,1)}, u32[]{:S(2)}, u32[]{:S(2)}) async-start(bf16[56,64,256]{2,1,0:T(8,128)(2,1)} %scatter_fusion), calls=%async_computation.2 | async-start | bytes 3670016 | tf_op jit(solution)/shard_map/all_to_all | solution.py:227
  168.2 6.0 %copy-start.6 = (bf16[4,3,64,4,256]{4,2,1,3,0:T(8,128)(2,1)S(1)}, bf16[4,3,64,4,256]{4,2,1,3,0:T(8,128)(2,1)}, u32[]{:S(2)}) copy-start(bf16[4,3,64,4,256]{4,2,1,3,0:T(8,128)(2,1)} %copy-done.4) | copy-start | bytes 4718596
  168.5 6.9 %copy-start.19 = (f32[6,64,4,256]{3,1,2,0:T(8,128)}, f32[6,64,4,256]{3,1,2,0:T(8,128)S(1)}, u32[]{:S(2)}) copy-start(f32[6,64,4,256]{3,1,2,0:T(8,128)S(1)} %get-tuple-element.29) | copy-start | bytes 4718596
  168.5 6.2 %copy-start.10 = (bf16[4,4,3,64,128]{4,3,2,1,0:T(8,128)(2,1)S(1)}, bf16[4,4,3,64,128]{4,3,2,1,0:T(8,128)(2,1)}, u32[]{:S(2)}) copy-start(bf16[4,4,3,64,128]{4,3,2,1,0:T(8,128)(2,1)} %copy-done.9) | copy-start | bytes 2359300
  168.7 17.6 %collective-permute-start.2 = (bf16[64,1024]{1,0:T(8,128)(2,1)S(1)}, bf16[64,1024]{1,0:T(8,128)(2,1)S(1)}, u32[]{:S(2)}, u32[]{:S(2)}) collective-permute-start(bf16[64,1024]{1,0:T(8,128)(2,1)S(1)} %bitcast.199), channel_id=1, source_target_pairs={{0,4},{4,8},{8,12},{12,16},{16,20},{20,24},{24,28},{1,5},{5,9},{9,... | collective-permute-start | bytes 393224 | tf_op jit(solution)/shard_map/ppermute | solution.py:20
  172.8 2.3 copy-start.21
  172.8 13.6 %collective-permute-start.3 = (bf16[64,1024]{1,0:T(8,128)(2,1)S(1)}, bf16[64,1024]{1,0:T(8,128)(2,1)S(1)}, u32[]{:S(2)}, u32[]{:S(2)}) collective-permute-start(bf16[64,1024]{1,0:T(8,128)(2,1)S(1)} %bitcast.201), channel_id=1, source_target_pairs={{4,0},{8,4},{12,8},{16,12},{20,16},{24,20},{28,24},{5,1},{9,5},{13... | collective-permute-start | bytes 393224 | tf_op jit(solution)/shard_map/ppermute | solution.py:22
  242.4 32.2 %copy-start.1 = (s32[16,32,3]{1,0,2:T(8,128)S(1)}, s32[16,32,3]{1,0,2:T(8,128)}, u32[]{:S(2)}) copy-start(s32[16,32,3]{1,0,2:T(8,128)} %param.16) | copy-start | bytes 18436
Sparse Core Ops, SparseCore 0:
  9.6 25.2 all-gather.4
  37.6 88.3 all-gather.2
  142.9 83.1 all-reduce.5
  228.6 43.7 reduce-scatter.1
